TPU v7x, 512 devices: a whole 4x4x16 slice. The times are simulated.
512 devices in a mesh: seq: 64 (over z, y), chan: 8 (over x, core).
Axes of the slice: x: 4, y: 4, z: 16, core: 2. Of those that a mesh axis runs over, the one named last changes fastest.
Arguments:
- query: bfloat16 [8192, 4096], P('seq', 'chan'), may hold values from -6 to 6
- key: bfloat16 [8192, 4096], P('seq', 'chan'), may hold values from -6 to 6
- value: bfloat16 [8192, 4096], P('seq', 'chan'), may hold values from -6 to 6
- residual: bfloat16 [8192, 4096], P('seq', 'chan'), may hold values from -6 to 6
- short_taps: float32 [3, 3, 4096], P(None, None, 'chan'), may hold values from -3.5 to 3.5
- decay: float32 [16, 4096], P(None, 'chan'), may hold values from 0.00012207031 to 0.05
- residue: float32 [16, 4096], P(None, 'chan'), may hold values from -3 to 3
- skip_gain: float32 [4096], P('chan'), may hold values from 0.5 to 1.5
- segments: int32 [64], replicated, may hold values from 0 to 7, never falling along the last dimension, each value on 1 to 32 neighbouring positions
- out_weight: bfloat16 [4096, 4096], P('seq', 'chan'), may hold values from -0.09375 to 0.09375
Outputs:
- block_out: bfloat16 [8192, 4096], P('seq', 'chan')
Inputs may be any that keep to these rules, and one draw needn't show every extreme that they name: `segments`: contig ids of the tiles never fall; each contig covers 1 to 32 tiles, one exactly 32.
All inputs are finite; a program needn't handle non-finite values.
Results may differ from a plain program's by a relative error of at most 0.0063.
Values may be sent and summed in bfloat16 or wider, within the bound.
A program may use at most 64 MiB of HBM per device.

v0:
```python
import jax
import jax.numpy as jnp
from jax import lax
from jax.sharding import PartitionSpec as P

SHORT = 3
TILE = 128


def from_behind(shard, axis, by):
    size = lax.axis_size(axis)
    pairs = [(i, i + by) for i in range(size) if 0 <= i + by < size]
    return lax.ppermute(shard, axis, pairs)


def pair_combine(earlier, later):
    return (earlier[0] * later[0], later[0] * earlier[1] + later[1])


def phase_one(blocks, same, decay, gain):
    width, count, tile = blocks.shape
    steps = jnp.arange(tile, dtype=jnp.float32)
    table = jnp.einsum(
        "mc,mct->ct", gain, jnp.exp(-decay[:, :, None] * steps), precision=lax.Precision.HIGHEST
    )
    places = jnp.arange(tile, dtype=jnp.int32)
    lagged = places[:, None] - places[None, :]
    toeplitz = jnp.where(
        lagged[None] >= 0, table[:, jnp.clip(lagged, 0, tile - 1)], jnp.float32(0.0)
    )
    inside = jnp.einsum("cts,cbs->cbt", toeplitz, blocks, precision=lax.Precision.HIGH)
    tail = jnp.exp(-decay[:, :, None] * (tile - 1 - steps))
    local = jnp.einsum("mcs,cbs->bmc", tail, blocks, precision=lax.Precision.HIGH)
    factor = jnp.exp(-decay * tile)[None] * same[:, None, None]
    cums, states = lax.associative_scan(pair_combine, (factor, local), axis=0)
    return (inside, states, cums)


def phase_two(inside, states, cums, carry, same, decay, gain, skip, blocks):
    tile = blocks.shape[2]
    steps = jnp.arange(tile, dtype=jnp.float32)
    ending = states + cums * carry[None]
    entering = jnp.concatenate([carry[None], ending[:-1]], axis=0)
    reach = gain[:, :, None] * jnp.exp(-decay[:, :, None] * (steps + 1.0))
    cross = jnp.einsum("mct,bmc->cbt", reach, entering, precision=lax.Precision.HIGHEST)
    return inside + cross * same[None, :, None] + skip[:, None, None] * blocks


def short_mix(stream, rim, taps, seg_ext, rows):
    extended = jnp.concatenate([rim, stream], axis=0).astype(jnp.float32)
    own = seg_ext[SHORT - 1 :]
    total = jnp.zeros(stream.shape, jnp.float32)
    for tap in range(SHORT):
        live = seg_ext[SHORT - 1 - tap : SHORT - 1 - tap + rows] == own
        moved = extended[SHORT - 1 - tap : SHORT - 1 - tap + rows]
        total = total + jnp.where(live[:, None], moved * taps[tap][None, :], jnp.float32(0.0))
    return total


def per_device(
    query, key, value, residual, short_taps, decay, residue, skip_gain, segments, out_weight
):
    rows, width = query.shape
    device = lax.axis_index("seq")
    rims = from_behind(
        (query[rows - SHORT + 1 :], key[rows - SHORT + 1 :], value[rows - SHORT + 1 :]), "seq", 1
    )
    global_rows = jnp.arange(rows + SHORT - 1, dtype=jnp.int32) - (SHORT - 1) + device * rows
    seg_ext = segments[jnp.clip(jnp.floor_divide(global_rows, TILE), 0, segments.shape[0] - 1)]
    q_mixed = short_mix(query, rims[0], short_taps[0], seg_ext, rows)
    k_mixed = short_mix(key, rims[1], short_taps[1], seg_ext, rows)
    v_mixed = short_mix(value, rims[2], short_taps[2], seg_ext, rows)
    mixed_input = (k_mixed * v_mixed).astype(jnp.bfloat16)
    gain = residue * jnp.sqrt(decay)
    by_channel = mixed_input.T
    spread = lax.all_to_all(by_channel, "seq", split_axis=0, concat_axis=1, tiled=True)
    share = spread.shape[0]
    length = spread.shape[1]
    start = device * share
    rate_part = lax.dynamic_slice_in_dim(decay, start, share, 1)
    gain_part = lax.dynamic_slice_in_dim(gain, start, share, 1)
    skip_part = lax.dynamic_slice_in_dim(skip_gain, start, share, 0)
    same = jnp.concatenate(
        [jnp.zeros((1,), jnp.float32), (segments[1:] == segments[:-1]).astype(jnp.float32)]
    )
    blocks = spread.astype(jnp.float32).reshape(share, length // TILE, TILE)
    inside, states, cums = phase_one(blocks, same, rate_part, gain_part)
    carry = jnp.zeros((decay.shape[0], share), jnp.float32)
    long_out = phase_two(inside, states, cums, carry, same, rate_part, gain_part, skip_part, blocks)
    long_cols = long_out.reshape(share, length).astype(jnp.bfloat16)
    returned = lax.all_to_all(long_cols, "seq", split_axis=1, concat_axis=0, tiled=True)
    gated = (q_mixed * returned.T.astype(jnp.float32)).astype(jnp.bfloat16)
    features = lax.all_gather(gated, "chan", axis=1, tiled=True)
    projected = jnp.dot(
        features,
        lax.all_gather(out_weight, "seq", axis=0, tiled=True),
        preferred_element_type=jnp.float32,
    )
    return (residual.astype(jnp.float32) + projected).astype(jnp.bfloat16)


def solution(mesh):
    placed = (
        P("seq", "chan"),
        P("seq", "chan"),
        P("seq", "chan"),
        P("seq", "chan"),
        P(None, None, "chan"),
        P(None, "chan"),
        P(None, "chan"),
        P("chan"),
        P(),
        P("seq", "chan"),
    )
    return jax.shard_map(
        per_device, mesh=mesh, in_specs=placed, out_specs=P("seq", "chan"), check_vma=False
    )
```

profile of v0, /device:TPU:2, one launch (start us, length us, event | category | flops | bytes accessed | tf_op | source)
XLA Modules:
  0.0 345.9 jit_solution(14340222937160160731)
XLA Ops:
  6.5 0.7 slice.291
  7.4 3.5 %collective-permute-start.1 = (bf16[2,512]{0,1:T(8,128)(2,1)S(1)}, bf16[2,512]{0,1:T(8,128)(2,1)S(1)}, u32[]{:S(2)}, u32[]{:S(2)}) collective-permute-start(bf16[2,512]{0,1:T(8,128)(2,1)S(1)} %copy.66), channel_id=1, source_target_pairs={{0,8},{8,16},{16,24},{24,32},{32,40},{40,48},{48,56},{56,64},{64,7... | collective-permute-start | bytes 6152 | tf_op jit(solution)/shard_map/ppermute | solution.py:13
  10.9 0.7 slice.298
  11.8 3.5 %collective-permute-start.2 = (bf16[2,512]{0,1:T(8,128)(2,1)S(1)}, bf16[2,512]{0,1:T(8,128)(2,1)S(1)}, u32[]{:S(2)}, u32[]{:S(2)}) collective-permute-start(bf16[2,512]{0,1:T(8,128)(2,1)S(1)} %copy.68), channel_id=1, source_target_pairs={{0,8},{8,16},{16,24},{24,32},{32,40},{40,48},{48,56},{56,64},{64,7... | collective-permute-start | bytes 6152 | tf_op jit(solution)/shard_map/ppermute | solution.py:13
  15.3 0.9 fusion.50
  16.2 0.8 slice_compare_fusion
  17.0 1.9 gather_fusion
  19.0 0.8 constant_dynamic-slice_fusion
  20.2 1.0 copy.67
  21.3 1.0 copy.69
  22.3 0.6 slice.309
  22.9 0.6 slice.313
  23.5 0.6 slice.308
  24.6 1.4 fusion.27
  26.0 17.8 %all-to-all-start = ((bf16[64,8,128]{2,1,0:T(8,128)(2,1)}), bf16[64,8,128]{2,1,0:T(8,128)(2,1)S(1)}, u32[]{:S(2)}, u32[]{:S(2)}) async-start(bf16[64,8,128]{2,1,0:T(8,128)(2,1)} %fusion.27), calls=%async_computation | async-start | bytes 262144 | tf_op jit(solution)/shard_map/all_to_all | solution.py:76
  43.9 54.5 %gather_fusion.1 = f32[16384,8]{1,0:T(8,128)} fusion(f32[8,128]{0,1:T(8,128)S(1)} %copy.80, s32[16384]{0:T(1024)S(1)} %fusion.31), kind=kCustom, calls=%fused_computation.1 | custom fusion | bytes 1114112 | tf_op jit(solution)/shard_map/gather | solution.py:29
  98.4 5.1 %copy.72 = f32[128,128,8]{1,0,2:T(8,128)S(1)} copy(f32[128,128,8]{2,1,0:T(8,128)} %bitcast.49) | data formatting | bytes 1048576 | tf_op jit(solution)/shard_map/gather | solution.py:29
  103.5 0.8 dynamic_slice.11
  104.3 0.3 convolution_bitcast_fusion
  104.7 0.6 slice.310
  105.3 0.6 slice.311
  105.9 0.3 slice.316
  106.2 0.3 slice.317
  106.6 0.3 slice.315
  106.9 0.3 slice.319
  107.5 0.2 slice.323
  107.7 0.2 slice.321
  107.9 0.2 slice.325
  109.8 0.2 slice.320
  110.2 0.3 slice.314
  110.5 0.3 slice.347
  110.8 0.6 slice.349
  111.4 0.6 pad.78
  112.0 0.6 pad.90
  112.7 0.6 pad.77
  113.3 0.6 pad.89
  114.0 0.6 pad.91
  114.6 0.6 pad.92
  115.3 0.6 pad.79
  115.9 0.6 pad.80
  116.7 0.7 pad.93
  117.3 0.7 pad.94
  118.0 0.7 pad.82
  118.8 0.7 pad.81
  119.7 0.8 pad.95
  120.5 0.8 pad.96
  121.3 1.1 pad.172
  122.5 0.8 pad.83
  123.3 0.8 pad.84
  124.1 1.1 pad.173
  125.3 1.1 pad.133
  126.4 1.1 pad.131
  127.5 0.5 fusion.4
  128.0 0.7 fusion.2
  128.7 0.7 copy.74
  129.4 14.9 %all-to-all-start.1 = ((bf16[8,64,128]{2,0,1:T(8,128)(2,1)}), bf16[8,64,128]{2,0,1:T(8,128)(2,1)S(1)}, u32[]{:S(2)}, u32[]{:S(2)}) async-start(bf16[8,64,128]{2,0,1:T(8,128)(2,1)} %copy.74), calls=%async_computation.1 | async-start | bytes 262144 | tf_op jit(solution)/shard_map/all_to_all | solution.py:91
  144.6 3.5 %collective-permute-start = (bf16[2,512]{0,1:T(8,128)(2,1)S(1)}, bf16[2,512]{0,1:T(8,128)(2,1)S(1)}, u32[]{:S(2)}, u32[]{:S(2)}) collective-permute-start(bf16[2,512]{0,1:T(8,128)(2,1)S(1)} %copy.64), channel_id=1, source_target_pairs={{0,8},{8,16},{16,24},{24,32},{32,40},{40,48},{48,56},{56,64},{64,7... | collective-permute-start | bytes 6152 | tf_op jit(solution)/shard_map/ppermute | solution.py:13
  148.2 2.6 collective-permute-done
  151.0 10.4 %all-to-all-done.1 = bf16[8,64,128]{2,0,1:T(8,128)(2,1)S(1)} async-done(((bf16[8,64,128]{2,0,1:T(8,128)(2,1)}), bf16[8,64,128]{2,0,1:T(8,128)(2,1)S(1)}, u32[]{:S(2)}, u32[]{:S(2)}) %all-to-all-start.1) | async-done | bytes 131104 | tf_op jit(solution)/shard_map/all_to_all | solution.py:91
  161.4 1.1 fusion.20
  162.6 0.7 all-gather.5.cloned.1.call-update
  163.3 21.1 %all-gather.3.cloned.1.call-done = bf16[128,4096]{0,1:T(8,128)(2,1)} async-done(((bf16[128,512]{0,1:T(8,128)(2,1)}), bf16[128,4096]{0,1:T(8,128)(2,1)}) %all-gather.3.cloned.1.call-update) | async-done | bytes 1048592 | tf_op jit(solution)/shard_map/all_gather | solution.py:93
  184.4 150.8 %all-gather.5.cloned.1.call-done = bf16[4096,512]{1,0:T(8,128)(2,1)} async-done(((bf16[64,512]{1,0:T(8,128)(2,1)}), bf16[4096,512]{1,0:T(8,128)(2,1)}) %all-gather.5.cloned.1.call-update) | async-done | bytes 4194320 | tf_op jit(solution)/shard_map/all_gather | solution.py:96
  335.2 3.9 %fusion.3 = bf16[128,512]{1,0:T(8,128)(2,1)} fusion(bf16[128,4096]{0,1:T(8,128)(2,1)} %all-gather.3.cloned.1.call-done, bf16[4096,512]{1,0:T(8,128)(2,1)} %all-gather.5.cloned.1.call-done, bf16[128,512]{1,0:T(8,128)(2,1)S(1)} %copy-done.1), kind=kOutput, calls=%fused_computation.7 | convolution fusion | flops 537067520 | bytes 5505024 | tf_op jit(solution)/shard_map/dot_general | solution.py:94
  (75 shorter events, 5.0 us)
Async XLA Ops:
  7.4 16.9 %collective-permute-start.1 = (bf16[2,512]{0,1:T(8,128)(2,1)S(1)}, bf16[2,512]{0,1:T(8,128)(2,1)S(1)}, u32[]{:S(2)}, u32[]{:S(2)}) collective-permute-start(bf16[2,512]{0,1:T(8,128)(2,1)S(1)} %copy.66), channel_id=1, source_target_pairs={{0,8},{8,16},{16,24},{24,32},{32,40},{40,48},{48,56},{56,64},{64,7... | collective-permute-start | bytes 6152 | tf_op jit(solution)/shard_map/ppermute | solution.py:13
  11.8 12.6 %collective-permute-start.2 = (bf16[2,512]{0,1:T(8,128)(2,1)S(1)}, bf16[2,512]{0,1:T(8,128)(2,1)S(1)}, u32[]{:S(2)}, u32[]{:S(2)}) collective-permute-start(bf16[2,512]{0,1:T(8,128)(2,1)S(1)} %copy.68), channel_id=1, source_target_pairs={{0,8},{8,16},{16,24},{24,32},{32,40},{40,48},{48,56},{56,64},{64,7... | collective-permute-start | bytes 6152 | tf_op jit(solution)/shard_map/ppermute | solution.py:13
  26.0 78.3 %all-to-all-start = ((bf16[64,8,128]{2,1,0:T(8,128)(2,1)}), bf16[64,8,128]{2,1,0:T(8,128)(2,1)S(1)}, u32[]{:S(2)}, u32[]{:S(2)}) async-start(bf16[64,8,128]{2,1,0:T(8,128)(2,1)} %fusion.27), calls=%async_computation | async-start | bytes 262144 | tf_op jit(solution)/shard_map/all_to_all | solution.py:76
  115.2 29.2 %copy-start = (bf16[128,512]{1,0:T(8,128)(2,1)S(1)}, bf16[128,512]{1,0:T(8,128)(2,1)}, u32[]{:S(2)}) copy-start(bf16[128,512]{1,0:T(8,128)(2,1)} %param.10) | copy-start | bytes 393220
  119.5 215.7 %copy-start.1 = (bf16[128,512]{1,0:T(8,128)(2,1)S(1)}, bf16[128,512]{1,0:T(8,128)(2,1)}, u32[]{:S(2)}) copy-start(bf16[128,512]{1,0:T(8,128)(2,1)} %param.13) | copy-start | bytes 393220
  129.4 32.0 %all-to-all-start.1 = ((bf16[8,64,128]{2,0,1:T(8,128)(2,1)}), bf16[8,64,128]{2,0,1:T(8,128)(2,1)S(1)}, u32[]{:S(2)}, u32[]{:S(2)}) async-start(bf16[8,64,128]{2,0,1:T(8,128)(2,1)} %copy.74), calls=%async_computation.1 | async-start | bytes 262144 | tf_op jit(solution)/shard_map/all_to_all | solution.py:91
  144.4 40.0 %all-gather.3.cloned.1.call-start = ((), (), s32[]{:S(2)}) async-start(), calls=%async_computation.2 | async-start | bytes 1179648 | tf_op jit(solution)/shard_map/all_gather | solution.py:93
  144.6 6.2 %collective-permute-start = (bf16[2,512]{0,1:T(8,128)(2,1)S(1)}, bf16[2,512]{0,1:T(8,128)(2,1)S(1)}, u32[]{:S(2)}, u32[]{:S(2)}) collective-permute-start(bf16[2,512]{0,1:T(8,128)(2,1)S(1)} %copy.64), channel_id=1, source_target_pairs={{0,8},{8,16},{16,24},{24,32},{32,40},{40,48},{48,56},{56,64},{64,7... | collective-permute-start | bytes 6152 | tf_op jit(solution)/shard_map/ppermute | solution.py:13
  162.5 172.6 %all-gather.5.cloned.1.call-start = ((), (), s32[]{:S(2)}) async-start(), calls=%async_computation.3 | async-start | bytes 4259840 | tf_op jit(solution)/shard_map/all_gather | solution.py:96
Sparse Core Ops, SparseCore 0:
  162.6 21.7 all-gather.2
  187.3 147.7 all-gather.4
where the time goes:
time: 347 us; the launch traced here: 346 us
  waiting for transfers between devices  186 us (54%)
  local copies, waits for them, and re-layouts  91.1 us (26%)
  starting transfers between devices  43.3 us (12%)
  between operations  14.1 us (4%)
  other arithmetic  6.41 us (2%)
  matrix products  5.37 us (2%)
    all_gather x1, waiting for transfers between devices, per_device(): lax.all_gather(out_weight, 'seq', axis=0, tiled=True)  151 us
    gather x2, local copies, waits for them, and re-layouts, phase_one(): table[:, jnp.clip(lagged, 0, tile - 1)]  59.6 us
    all_gather x1, waiting for transfers between devices, per_device(): features = lax.all_gather(gated, 'chan', axis=1, tiled=True)  21.1 us
    all_to_all x1, starting transfers between devices, per_device(): lax.all_to_all(by_channel, 'seq', split_axis=0, concat_axis=1, tiled=True)  17.8 us
    all_to_all x1, starting transfers between devices, per_device(): lax.all_to_all(long_cols, 'seq', split_axis=1, concat_axis=0, tiled=True)  14.9 us
    pad x16, local copies, waits for them, and re-layouts, phase_one(): cums, states = lax.associative_scan(pair_combine, (factor, local), axis=0)  10.5 us
    ppermute x3, starting transfers between devices, from_behind(): return lax.ppermute(shard, axis, pairs)  10.5 us
    all_to_all x1, waiting for transfers between devices, per_device(): lax.all_to_all(long_cols, 'seq', split_axis=1, concat_axis=0, tiled=True)  10.4 us
  transfers between devices with their start and end apart: 7, of which 4 were waited for; matrix products, arithmetic and copies ran while one was open for 20% of the time, Pallas kernels for 0%

commit v1 on v0

v1 whole, which is shorter than its diff:
```python
import jax
import jax.numpy as jnp
from jax import lax
from jax.experimental import pallas as pl
from jax.experimental.pallas import tpu as pltpu
from jax.sharding import PartitionSpec as P

MESH = pl.DeviceIdType.MESH
BF = jnp.bfloat16
F32 = jnp.float32

NZ, NY, NX = 16, 4, 4
TILE = 128
MODES = 16
CH = 128
ROWS = NY * TILE
CHUNK = ROWS // 8
BACK = 8

W_FIRST = ((4, 12), (-4, 4), (8, 8), (1, 15), (-1, 1), (2, 14))
W_NEXT = ((4, 1), (8, 1), (12, 1), (4, -1), (8, -1), (12, -1), (4, 2), (4, -2), (8, -2))


def kernel(
    seg_ref, q_ref, k_ref, v_ref, res_ref, taps_ref, decay_ref, residue_ref, skip_ref, w_ref,
    out_ref,
    stage, rbuf, rim, fq, fk, fv, prm, xs, qs, ys, dtab, gtab, atab, ctab, asend, arecv,
    gbuf, xbuf, wbuf, psend, precv, own,
    y_send, y_recv, rim_send, rim_recv, a_send, a_recv, x_send, x_recv, f_send, f_recv,
    w_send, w_recv, p_send, p_recv,
):
    seq = lax.axis_index("seq")
    chan = lax.axis_index("chan")
    z, y = seq // NY, seq % NY
    x, core = chan // 2, chan % 2

    def dev(dz=0, dy=0, dx=0, dc=0, toy=None):
        yy = lax.rem(y + dy + NY, NY) if toy is None else toy
        return (
            lax.rem(z + dz + NZ, NZ) * NY + yy,
            lax.rem(x + dx + NX, NX) * 2 + (core if dc == 0 else 1 - core),
        )

    barrier = pltpu.get_barrier_semaphore()

    def greet(where):
        pl.semaphore_signal(barrier, inc=1, device_id=where, device_id_type=MESH)

    for j in range(1, NY):
        greet(dev(dy=j))
    for j in range(1, NZ):
        greet(dev(dz=j))
    for j in range(1, NX):
        greet(dev(dx=j))
    greet(dev(dc=1))

    @pl.when(y == NY - 1)
    def _():
        for t in range(NY - 1):
            greet(dev(dz=1, toy=t))

    @pl.when(y != NY - 1)
    def _():
        greet(dev(dz=-1, toy=NY - 1))

    src = lax.broadcasted_iota(jnp.int32, (512, 512), 0)
    dst = lax.broadcasted_iota(jnp.int32, (512, 512), 1)
    wanted = ((dst >> 6) & 1) * 256 + (dst >> 7) * 64 + (dst & 63)
    perm = jnp.where(src == wanted, 1.0, 0.0).astype(BF)
    for s, ref in enumerate((q_ref, k_ref, v_ref)):
        moved = jnp.dot(ref[...], perm, preferred_element_type=F32).astype(BF)
        for t in range(NY):
            stage[t, s] = moved[:, t * CH : (t + 1) * CH]

    pl.semaphore_wait(barrier, 22 + jnp.where(y == NY - 1, 3, 1))

    y_copies = []
    for j in range(1, NY):
        to = lax.rem(y + j, NY)
        cp = pltpu.make_async_remote_copy(
            src_ref=stage.at[to], dst_ref=rbuf.at[y], send_sem=y_send.at[j - 1],
            recv_sem=y_recv.at[j - 1], device_id=dev(dy=j), device_id_type=MESH)
        cp.start()
        y_copies.append(cp)

    def rim_copy(t):
        return pltpu.make_async_remote_copy(
            src_ref=stage.at[t, :, pl.ds(TILE - 16, 16), :], dst_ref=rim, send_sem=rim_send.at[t],
            recv_sem=rim_recv, device_id=dev(dz=1, toy=t), device_id_type=MESH)

    @pl.when(y == NY - 1)
    def _():
        for t in range(NY):
            rim_copy(t).start()

    w_copies = []

    def send_w(source, tile, dz, number):
        cp = pltpu.make_async_remote_copy(
            src_ref=source, dst_ref=wbuf.at[tile], send_sem=w_send.at[len(w_copies)],
            recv_sem=w_recv.at[number], device_id=dev(dz=dz), device_id_type=MESH)
        cp.start()
        w_copies.append(cp)

    def wait_w(number):
        tile = lax.rem(z + number, NZ)
        pltpu.make_async_remote_copy(
            src_ref=w_ref, dst_ref=wbuf.at[tile], send_sem=w_send.at[0],
            recv_sem=w_recv.at[number], device_id=dev(dz=1), device_id_type=MESH).wait_recv()

    for dz, number in W_FIRST:
        send_w(w_ref, z, dz, number)
    wbuf[z] = w_ref[...]

    prm[0:16] = decay_ref[...]
    prm[16:32] = residue_ref[...]
    for s in range(3):
        prm[32 + 3 * s : 35 + 3 * s] = taps_ref[s]
    prm[41:42] = skip_ref[...]
    prm[42:48] = jnp.zeros((6, 512), F32)
    lane = lax.broadcasted_iota(jnp.int32, (512, CH), 1)
    row = lax.broadcasted_iota(jnp.int32, (512, CH), 0)
    pick = jnp.where(row == ((lane >> 6) & 1) * 256 + y * 64 + (lane & 63), 1.0, 0.0).astype(F32)
    mine = jnp.dot(
        prm[...], pick, precision=lax.Precision.HIGHEST, preferred_element_type=F32)
    rate = mine[0:16]
    gain = mine[16:32] * jnp.sqrt(rate)
    taps = [[jnp.broadcast_to(mine[32 + 3 * s + j : 33 + 3 * s + j], (8, CH)) for j in range(3)]
            for s in range(3)]
    skip = jnp.broadcast_to(mine[41:42], (8, CH))

    one = jnp.float32(1.0)
    zero = jnp.float32(0.0)
    seg = [seg_ref[z * NY + t] for t in range(NY)]
    before = seg_ref[jnp.maximum(z * NY - 1, 0)]
    same = [jnp.where(jnp.logical_and(z > 0, before == seg[0]), one, zero)]
    for t in range(1, NY):
        same.append(jnp.where(seg[t] == seg[t - 1], one, zero))
    ends = [jnp.where(seg[t] == seg[NY - 1], one, zero) for t in range(NY)]
    starts = [jnp.where(seg[t] == seg[0], one, zero) for t in range(NY)]
    sub = lax.broadcasted_iota(jnp.int32, (8, CH), 0)

    def by_tile(values):
        total = jnp.full((8, CH), values[0], F32)
        for t in range(1, NY):
            total = jnp.where((sub >> 1) == t, values[t], total)
        return total

    joined = jnp.where((sub & 1) == 1, one, by_tile(same))
    subf = sub.astype(F32)
    rate8 = jnp.broadcast_to(rate[:, None, :], (MODES, 8, CH))
    gain8 = jnp.broadcast_to(gain[:, None, :], (MODES, 8, CH))
    dtab[...] = jnp.exp(-rate8)
    gtab[...] = gain8
    atab[...] = jnp.exp(-rate8 * (CHUNK * (7.0 - subf))[None]) * by_tile(ends)[None]
    ctab[...] = gain8 * jnp.exp(-rate8 * (CHUNK * subf)[None]) * by_tile(starts)[None]
    chunk_decay = jnp.exp(-rate8 * float(CHUNK)) * joined[None]

    streams = (fq, fk, fv)
    here = pl.multiple_of(8 + y * TILE, 8)
    for s in range(3):
        streams[s][pl.ds(here, TILE)] = stage[y, s].astype(F32)
    for j in range(1, NY):
        y_copies[j - 1].wait_recv()
        origin = lax.rem(y - j + NY, NY)
        at = pl.multiple_of(8 + origin * TILE, 8)
        for s in range(3):
            streams[s][pl.ds(at, TILE)] = rbuf[origin, s].astype(F32)
    rim_copy(0).wait_recv()
    for s in range(3):
        streams[s][0:8] = rim[s].astype(F32)[8:16]

    def load(s, b):
        return streams[s][pl.ds(8 + b, 8, stride=CHUNK), :]

    def mix(now, last, older):
        out = []
        for s in range(3):
            out.append(now[s] * taps[s][0] + last[s] * taps[s][1] + older[s] * taps[s][2])
        return out[0], (out[1] * out[2]).astype(BF).astype(F32)

    def keep(b, mixed):
        qs[b] = mixed[0]
        xs[b] = mixed[1]
        return mixed[1]

    m2 = [load(s, -2) * joined for s in range(3)]
    m1 = [load(s, -1) * joined for s in range(3)]
    f0 = [load(s, 0) for s in range(3)]
    f1 = [load(s, 1) for s in range(3)]
    d16 = dtab[...]
    x0 = keep(0, mix(f0, m1, m2))
    x1 = keep(1, mix(f1, f0, m1))
    h = x0[None] * d16 + x1[None]

    def first_pass(b, carry):
        h, last, older = carry
        now = [load(s, b) for s in range(3)]
        xb = keep(b, mix(now, last, older))
        return (h * dtab[...] + xb[None], now, last)

    h, _, _ = lax.fori_loop(2, CHUNK, first_pass, (h, f1, f0), unroll=2)

    asend[...] = jnp.sum(h * atab[...], axis=1).astype(BF)
    a_copies = []
    for k in range(1, BACK + 1):
        cp = pltpu.make_async_remote_copy(
            src_ref=asend, dst_ref=arecv.at[k - 1], send_sem=a_send.at[k - 1],
            recv_sem=a_recv.at[k - 1], device_id=dev(dz=k), device_id_type=MESH)
        cp.start()
        a_copies.append(cp)

    span = 1
    factor = chunk_decay
    state = h
    while span < 8:
        state = state + jnp.where(sub[None] >= span, factor * pltpu.roll(state, span, 1), zero)
        factor = factor * pltpu.roll(factor, span, 1)
        span *= 2
    entering = jnp.where(sub[None] >= 1, pltpu.roll(state, 1, 1) * joined[None], zero)

    def second_pass(b, h):
        xb = xs[b]
        h = h * dtab[...] + xb[None]
        ys[b] = skip * xb + jnp.sum(h * gtab[...], axis=0)
        return h

    lax.fori_loop(0, CHUNK, second_pass, entering, unroll=2)

    for number in (4, 8, 12):
        wait_w(number)
    for number, dz in W_NEXT:
        tile = lax.rem(z + number, NZ)
        send_w(wbuf.at[tile], tile, dz, (number - dz) % NZ)

    carried = jnp.zeros((MODES, CH), F32)
    for k in range(1, BACK + 1):
        a_copies[k - 1].wait_recv()
        ending = seg_ref[jnp.maximum((z - k) * NY + NY - 1, 0)]
        live = jnp.where(jnp.logical_and(z >= k, ending == seg[0]), one, zero)
        weight = jnp.exp(-rate * float(ROWS * (k - 1))) * live
        carried = carried + weight * arecv[k - 1].astype(F32)

    def third_pass(b, e):
        e = e * dtab[...]
        long_out = (ys[b] + jnp.sum(e, axis=0)).astype(BF).astype(F32)
        gbuf[pl.ds(b, 8, stride=CHUNK), :] = qs[b] * long_out
        return e

    lax.fori_loop(0, CHUNK, third_pass, ctab[...] * carried[:, None, :], unroll=2)
    xbuf[chan] = gbuf[...].astype(BF)

    x_copies = []
    for i, move in enumerate((dict(dx=1), dict(dx=-1), dict(dx=2), dict(dc=1))):
        cp = pltpu.make_async_remote_copy(
            src_ref=xbuf.at[chan], dst_ref=xbuf.at[chan], send_sem=x_send.at[i],
            recv_sem=x_recv.at[i], device_id=dev(**move), device_id_type=MESH)
        cp.start()
        x_copies.append(cp)
    f_copies = []
    for i, dx in enumerate((-1, 1, 2)):
        x_copies[i].wait_recv()
        slot = lax.rem(x + dx + NX, NX) * 2 + core
        cp = pltpu.make_async_remote_copy(
            src_ref=xbuf.at[slot], dst_ref=xbuf.at[slot], send_sem=f_send.at[i],
            recv_sem=f_recv.at[i], device_id=dev(dc=1), device_id_type=MESH)
        cp.start()
        f_copies.append(cp)
    x_copies[3].wait_recv()
    for cp in f_copies:
        cp.wait_recv()
    for number in range(1, NZ):
        if number not in (4, 8, 12):
            wait_w(number)

    def project(at):
        rows = pl.ds(pl.multiple_of(at * TILE, TILE), TILE)
        total = jnp.zeros((TILE, 512), F32)
        for p in range(NX):
            left = jnp.concatenate([xbuf[2 * p, rows], xbuf[2 * p + 1, rows]], axis=1)
            right = wbuf[4 * p : 4 * p + 4].reshape(256, 512)
            total = total + jnp.dot(left, right, preferred_element_type=F32)
        return total

    p_copies = []
    for j in range(1, NY):
        psend[j - 1] = project(lax.rem(y + j, NY)).astype(BF)
        cp = pltpu.make_async_remote_copy(
            src_ref=psend.at[j - 1], dst_ref=precv.at[j - 1], send_sem=p_send.at[j - 1],
            recv_sem=p_recv.at[j - 1], device_id=dev(dy=j), device_id_type=MESH)
        cp.start()
        p_copies.append(cp)
    own[...] = project(y) + res_ref[...].astype(F32)
    for j in range(NY - 1):
        p_copies[j].wait_recv()
    out_ref[...] = (
        own[...] + precv[0].astype(F32) + precv[1].astype(F32) + precv[2].astype(F32)
    ).astype(BF)

    for cp in y_copies + w_copies + a_copies + x_copies + f_copies + p_copies:
        cp.wait_send()

    @pl.when(y == NY - 1)
    def _():
        for t in range(NY):
            rim_copy(t).wait_send()


def per_device(
    query, key, value, residual, short_taps, decay, residue, skip_gain, segments, out_weight
):
    vmem = pl.BlockSpec(memory_space=pltpu.VMEM)
    smem = pl.BlockSpec(memory_space=pltpu.SMEM)
    dma = pltpu.SemaphoreType.DMA
    scratch = [
        pltpu.VMEM((NY, 3, TILE, CH), BF),
        pltpu.VMEM((NY, 3, TILE, CH), BF),
        pltpu.VMEM((3, 16, CH), BF),
        pltpu.VMEM((8 + ROWS, CH), F32),
        pltpu.VMEM((8 + ROWS, CH), F32),
        pltpu.VMEM((8 + ROWS, CH), F32),
        pltpu.VMEM((48, 512), F32),
        pltpu.VMEM((CHUNK, 8, CH), F32),
        pltpu.VMEM((CHUNK, 8, CH), F32),
        pltpu.VMEM((CHUNK, 8, CH), F32),
        pltpu.VMEM((MODES, 8, CH), F32),
        pltpu.VMEM((MODES, 8, CH), F32),
        pltpu.VMEM((MODES, 8, CH), F32),
        pltpu.VMEM((MODES, 8, CH), F32),
        pltpu.VMEM((MODES, CH), BF),
        pltpu.VMEM((BACK, MODES, CH), BF),
        pltpu.VMEM((ROWS, CH), F32),
        pltpu.VMEM((2 * NX, ROWS, CH), BF),
        pltpu.VMEM((NZ, 64, 512), BF),
        pltpu.VMEM((NY - 1, TILE, 512), BF),
        pltpu.VMEM((NY - 1, TILE, 512), BF),
        pltpu.VMEM((TILE, 512), F32),
        dma((3,)), dma((3,)), dma((NY,)), dma,
        dma((BACK,)), dma((BACK,)), dma((4,)), dma((4,)), dma((3,)), dma((3,)),
        dma((15,)), dma((NZ,)), dma((3,)), dma((3,)),
    ]
    return pl.pallas_call(
        kernel,
        out_shape=jax.ShapeDtypeStruct((TILE, 512), BF),
        in_specs=[smem] + [vmem] * 9,
        out_specs=vmem,
        scratch_shapes=scratch,
        compiler_params=pltpu.CompilerParams(
            collective_id=0, has_side_effects=True, vmem_limit_bytes=32 * 1024 * 1024),
        name="hyena_block",
    )(segments, query, key, value, residual, short_taps, decay, residue,
      skip_gain.reshape(1, -1), out_weight)


def solution(mesh):
    placed = (
        P("seq", "chan"), P("seq", "chan"), P("seq", "chan"), P("seq", "chan"),
        P(None, None, "chan"), P(None, "chan"), P(None, "chan"), P("chan"), P(),
        P("seq", "chan"),
    )
    return jax.shard_map(
        per_device, mesh=mesh, in_specs=placed, out_specs=P("seq", "chan"), check_vma=False
    )
```

time: 347 us -> 67.1 us (0.19)
  the two profiles are of different devices: /device:TPU:2 before, /device:TPU:1 now
where the time goes in v1:
time: 67.1 us; the launch traced here: 66.6 us
  Pallas kernels  57.9 us (86%)
  local copies, waits for them, and re-layouts  8.7 us (13%)
    pallas_call x1, Pallas kernels, per_device(): pl.pallas_call(kernel, out_shape=jax.ShapeDtypeStruct((TILE, 512), BF), i...  57.9 us
    unnamed x21, local copies, waits for them, and re-layouts  8.7 us

profile of v1, /device:TPU:1, one launch (start us, length us, event | category | flops | bytes accessed | tf_op | source)
XLA Modules:
  0.0 66.6 jit_solution(6821252689407801653)
XLA Ops:
  0.0 0.0 copy-start.9
  0.0 0.7 copy-done.9
  0.7 0.0 copy-start
  0.7 0.9 %copy-done = bf16[128,512]{1,0:T(8,128)(2,1)S(1)} copy-done((bf16[128,512]{1,0:T(8,128)(2,1)S(1)}, bf16[128,512]{1,0:T(8,128)(2,1)}, u32[]{:S(2)}) %copy-start) | copy-done | bytes 131096
  1.6 0.0 copy-start.1
  1.6 0.9 %copy-done.1 = bf16[128,512]{1,0:T(8,128)(2,1)S(1)} copy-done((bf16[128,512]{1,0:T(8,128)(2,1)S(1)}, bf16[128,512]{1,0:T(8,128)(2,1)}, u32[]{:S(2)}) %copy-start.1) | copy-done | bytes 131096
  2.5 0.0 copy-start.2
  2.5 0.9 %copy-done.2 = bf16[128,512]{1,0:T(8,128)(2,1)S(1)} copy-done((bf16[128,512]{1,0:T(8,128)(2,1)S(1)}, bf16[128,512]{1,0:T(8,128)(2,1)}, u32[]{:S(2)}) %copy-start.2) | copy-done | bytes 131096
  3.4 0.0 copy-start.3
  3.4 0.9 %copy-done.3 = bf16[128,512]{1,0:T(8,128)(2,1)S(1)} copy-done((bf16[128,512]{1,0:T(8,128)(2,1)S(1)}, bf16[128,512]{1,0:T(8,128)(2,1)}, u32[]{:S(2)}) %copy-start.3) | copy-done | bytes 131096
  4.3 0.0 copy-start.4
  4.3 0.8 %copy-done.4 = bf16[64,512]{1,0:T(8,128)(2,1)S(1)} copy-done((bf16[64,512]{1,0:T(8,128)(2,1)S(1)}, bf16[64,512]{1,0:T(8,128)(2,1)}, u32[]{:S(2)}) %copy-start.4) | copy-done | bytes 65560
  5.1 0.0 copy-start.5
  5.1 0.8 %copy-done.5 = f32[16,512]{1,0:T(8,128)S(1)} copy-done((f32[16,512]{1,0:T(8,128)S(1)}, f32[16,512]{1,0:T(8,128)}, u32[]{:S(2)}) %copy-start.5) | copy-done | bytes 32792
  5.9 0.0 copy-start.6
  5.9 0.8 %copy-done.6 = f32[16,512]{1,0:T(8,128)S(1)} copy-done((f32[16,512]{1,0:T(8,128)S(1)}, f32[16,512]{1,0:T(8,128)}, u32[]{:S(2)}) %copy-start.6) | copy-done | bytes 32792
  6.6 0.0 copy-start.7
  6.6 0.7 %copy-done.7 = f32[3,3,512]{2,1,0:T(4,128)S(1)} copy-done((f32[3,3,512]{2,1,0:T(4,128)S(1)}, f32[3,3,512]{2,1,0:T(4,128)}, u32[]{:S(2)}) %copy-start.7) | copy-done | bytes 18456
  7.4 0.0 copy-start.8
  7.4 0.7 %copy-done.8 = f32[512]{0:T(512)S(1)} copy-done((f32[512]{0:T(512)S(1)}, f32[512]{0:T(512)}, u32[]{:S(2)}) %copy-start.8) | copy-done | bytes 2072
  8.1 57.9 %hyena_block.1 = bf16[128,512]{1,0:T(8,128)(2,1)S(1)} custom-call(s32[64]{0:T(128)S(1)} %copy-done.9, bf16[128,512]{1,0:T(8,128)(2,1)S(1)} %copy-done, bf16[128,512]{1,0:T(8,128)(2,1)S(1)} %copy-done.1, bf16[128,512]{1,0:T(8,128)(2,1)S(1)} %copy-done.2, bf16[128,512]{1,0:T(8,128)(2,1)S(1)} %copy-done.3, f32[3,3,512]{2,1,0:T(4,128)S(1)} %copy-done.7, ...), custom_call_target="tpu_custom_call" | custom-call | tf_op jit(solution)/shard_map/hyena_block/pallas_call | solution.py:342
  66.0 0.7 copy.12
Async XLA Ops:
  0.0 0.7 copy-start.9
  0.7 0.9 %copy-start = (bf16[128,512]{1,0:T(8,128)(2,1)S(1)}, bf16[128,512]{1,0:T(8,128)(2,1)}, u32[]{:S(2)}) copy-start(bf16[128,512]{1,0:T(8,128)(2,1)} %q_ref.1) | copy-start | bytes 393220
  1.6 0.9 %copy-start.1 = (bf16[128,512]{1,0:T(8,128)(2,1)S(1)}, bf16[128,512]{1,0:T(8,128)(2,1)}, u32[]{:S(2)}) copy-start(bf16[128,512]{1,0:T(8,128)(2,1)} %k_ref.1) | copy-start | bytes 393220
  2.5 0.9 %copy-start.2 = (bf16[128,512]{1,0:T(8,128)(2,1)S(1)}, bf16[128,512]{1,0:T(8,128)(2,1)}, u32[]{:S(2)}) copy-start(bf16[128,512]{1,0:T(8,128)(2,1)} %v_ref.1) | copy-start | bytes 393220
  3.4 0.9 %copy-start.3 = (bf16[128,512]{1,0:T(8,128)(2,1)S(1)}, bf16[128,512]{1,0:T(8,128)(2,1)}, u32[]{:S(2)}) copy-start(bf16[128,512]{1,0:T(8,128)(2,1)} %res_ref.1) | copy-start | bytes 393220
  4.3 0.8 %copy-start.4 = (bf16[64,512]{1,0:T(8,128)(2,1)S(1)}, bf16[64,512]{1,0:T(8,128)(2,1)}, u32[]{:S(2)}) copy-start(bf16[64,512]{1,0:T(8,128)(2,1)} %w_ref.1) | copy-start | bytes 196612
  5.1 0.8 %copy-start.5 = (f32[16,512]{1,0:T(8,128)S(1)}, f32[16,512]{1,0:T(8,128)}, u32[]{:S(2)}) copy-start(f32[16,512]{1,0:T(8,128)} %decay_ref.1) | copy-start | bytes 98308
  5.9 0.8 %copy-start.6 = (f32[16,512]{1,0:T(8,128)S(1)}, f32[16,512]{1,0:T(8,128)}, u32[]{:S(2)}) copy-start(f32[16,512]{1,0:T(8,128)} %residue_ref.1) | copy-start | bytes 98308
  6.6 0.7 %copy-start.7 = (f32[3,3,512]{2,1,0:T(4,128)S(1)}, f32[3,3,512]{2,1,0:T(4,128)}, u32[]{:S(2)}) copy-start(f32[3,3,512]{2,1,0:T(4,128)} %taps_ref.1) | copy-start | bytes 55300
  7.4 0.7 %copy-start.8 = (f32[512]{0:T(512)S(1)}, f32[512]{0:T(512)}, u32[]{:S(2)}) copy-start(f32[512]{0:T(512)} %param.17) | copy-start | bytes 6148

commit v2 on v1

--- a/solution.py
+++ b/solution.py
@@ -22,13 +22,24 @@
 
 
 def kernel(
-    seg_ref, q_ref, k_ref, v_ref, res_ref, taps_ref, decay_ref, residue_ref, skip_ref, w_ref,
+    seg_ref, q_hbm, k_hbm, v_hbm, res_hbm, taps_hbm, decay_hbm, residue_hbm, skip_hbm, w_hbm,
     out_ref,
+    q_ref, k_ref, v_ref, res_ref, taps_ref, decay_ref, residue_ref, skip_ref, w_ref,
     stage, rbuf, rim, fq, fk, fv, prm, xs, qs, ys, dtab, gtab, atab, ctab, asend, arecv,
     gbuf, xbuf, wbuf, psend, precv, own,
     y_send, y_recv, rim_send, rim_recv, a_send, a_recv, x_send, x_recv, f_send, f_recv,
-    w_send, w_recv, p_send, p_recv,
+    w_send, w_recv, p_send, p_recv, in_sem, go, zgo,
 ):
+    inputs = [
+        pltpu.make_async_copy(there, ref, in_sem.at[i])
+        for i, (there, ref) in enumerate((
+            (q_hbm, q_ref), (k_hbm, k_ref), (v_hbm, v_ref), (w_hbm, w_ref), (decay_hbm, decay_ref),
+            (residue_hbm, residue_ref), (taps_hbm, taps_ref), (skip_hbm, skip_ref),
+            (res_hbm, res_ref)))
+    ]
+    for cp in inputs:
+        cp.start()
+
     seq = lax.axis_index("seq")
     chan = lax.axis_index("chan")
     z, y = seq // NY, seq % NY
@@ -42,37 +53,93 @@
         )
 
     barrier = pltpu.get_barrier_semaphore()
-
-    def greet(where):
-        pl.semaphore_signal(barrier, inc=1, device_id=where, device_id_type=MESH)
-
-    for j in range(1, NY):
-        greet(dev(dy=j))
-    for j in range(1, NZ):
-        greet(dev(dz=j))
-    for j in range(1, NX):
-        greet(dev(dx=j))
-    greet(dev(dc=1))
-
-    @pl.when(y == NY - 1)
-    def _():
-        for t in range(NY - 1):
-            greet(dev(dz=1, toy=t))
+    hub = jnp.logical_and(chan == 0, y == 0)
+    hub_pair = jnp.logical_and(chan == 1, y == 0)
+
+    def greet(sem, where):
+        pl.semaphore_signal(sem, inc=1, device_id=where, device_id_type=MESH)
+
+    arecv[...] = jnp.zeros_like(arecv)
+    rim[...] = jnp.zeros_like(rim)
+
+    @pl.when(hub)
+    def _():
+        for j in range(NZ):
+            greet(barrier, dev(dz=j, dc=1))
+
+    @pl.when(jnp.logical_not(hub))
+    def _():
+        greet(barrier, (z * NY, 0))
+        for j in range(1, NZ):
+            greet(barrier, dev(dz=j))
 
     @pl.when(y != NY - 1)
     def _():
-        greet(dev(dz=-1, toy=NY - 1))
+        greet(barrier, dev(dz=-1, toy=NY - 1))
 
     src = lax.broadcasted_iota(jnp.int32, (512, 512), 0)
     dst = lax.broadcasted_iota(jnp.int32, (512, 512), 1)
     wanted = ((dst >> 6) & 1) * 256 + (dst >> 7) * 64 + (dst & 63)
     perm = jnp.where(src == wanted, 1.0, 0.0).astype(BF)
     for s, ref in enumerate((q_ref, k_ref, v_ref)):
+        inputs[s].wait()
         moved = jnp.dot(ref[...], perm, preferred_element_type=F32).astype(BF)
         for t in range(NY):
             stage[t, s] = moved[:, t * CH : (t + 1) * CH]
 
-    pl.semaphore_wait(barrier, 22 + jnp.where(y == NY - 1, 3, 1))
+    def send_w(source, tile, dz, number):
+        at = (number - 1) % NZ
+        pltpu.make_async_remote_copy(
+            src_ref=source, dst_ref=wbuf.at[tile], send_sem=w_send.at[at],
+            recv_sem=w_recv.at[number], device_id=dev(dz=dz), device_id_type=MESH).start()
+
+    def await_w(number):
+        return pltpu.make_async_remote_copy(
+            src_ref=w_ref, dst_ref=wbuf.at[lax.rem(z + number, NZ)], send_sem=w_send.at[number - 1],
+            recv_sem=w_recv.at[number], device_id=dev(dz=1), device_id_type=MESH)
+
+    def planes(moves):
+        @pl.when(jnp.logical_not(hub))
+        def _():
+            pl.semaphore_wait(
+                barrier, 15 + jnp.where(hub_pair, 16, jnp.where(y == NY - 1, 3, 0)))
+
+        @pl.when(hub_pair)
+        def _():
+            greet(zgo, dev(dc=1))
+
+        @pl.when(hub)
+        def _():
+            pl.semaphore_wait(zgo, 1)
+
+        for dz, number in moves:
+            send_w(w_ref, z, dz, number)
+
+    def next_tiles(moves):
+        for dz, number in moves:
+            send_w(w_ref, z, dz, number)
+        for number in (4, 8, 12):
+            await_w(number).wait_recv()
+        for number, dz in W_NEXT:
+            tile = lax.rem(z + number, NZ)
+            send_w(wbuf.at[tile], tile, dz, (number - dz) % NZ)
+
+    late = z >= NZ // 2
+    inputs[3].wait()
+
+    @pl.when(hub)
+    def _():
+        pl.semaphore_wait(barrier, NY * 2 * NX - 1)
+        for j in range(NY * 2 * NX - 1, 0, -1):
+            greet(go, (z * NY + j // (2 * NX), j % (2 * NX)))
+
+    @pl.when(late)
+    def _():
+        planes(W_FIRST)
+
+    @pl.when(jnp.logical_not(hub))
+    def _():
+        pl.semaphore_wait(go, 1)
 
     y_copies = []
     for j in range(1, NY):
@@ -88,30 +155,19 @@
             src_ref=stage.at[t, :, pl.ds(TILE - 16, 16), :], dst_ref=rim, send_sem=rim_send.at[t],
             recv_sem=rim_recv, device_id=dev(dz=1, toy=t), device_id_type=MESH)
 
-    @pl.when(y == NY - 1)
+    @pl.when(jnp.logical_not(late))
+    def _():
+        planes(W_FIRST[:3])
+
+    @pl.when(jnp.logical_and(y == NY - 1, z < NZ - 1))
     def _():
         for t in range(NY):
             rim_copy(t).start()
 
-    w_copies = []
-
-    def send_w(source, tile, dz, number):
-        cp = pltpu.make_async_remote_copy(
-            src_ref=source, dst_ref=wbuf.at[tile], send_sem=w_send.at[len(w_copies)],
-            recv_sem=w_recv.at[number], device_id=dev(dz=dz), device_id_type=MESH)
-        cp.start()
-        w_copies.append(cp)
-
-    def wait_w(number):
-        tile = lax.rem(z + number, NZ)
-        pltpu.make_async_remote_copy(
-            src_ref=w_ref, dst_ref=wbuf.at[tile], send_sem=w_send.at[0],
-            recv_sem=w_recv.at[number], device_id=dev(dz=1), device_id_type=MESH).wait_recv()
-
-    for dz, number in W_FIRST:
-        send_w(w_ref, z, dz, number)
     wbuf[z] = w_ref[...]
 
+    for cp in inputs[4:]:
+        cp.wait()
     prm[0:16] = decay_ref[...]
     prm[16:32] = residue_ref[...]
     for s in range(3):
@@ -166,7 +222,10 @@
         at = pl.multiple_of(8 + origin * TILE, 8)
         for s in range(3):
             streams[s][pl.ds(at, TILE)] = rbuf[origin, s].astype(F32)
-    rim_copy(0).wait_recv()
+    @pl.when(z > 0)
+    def _():
+        rim_copy(0).wait_recv()
+
     for s in range(3):
         streams[s][0:8] = rim[s].astype(F32)[8:16]
 
@@ -207,8 +266,13 @@
         cp = pltpu.make_async_remote_copy(
             src_ref=asend, dst_ref=arecv.at[k - 1], send_sem=a_send.at[k - 1],
             recv_sem=a_recv.at[k - 1], device_id=dev(dz=k), device_id_type=MESH)
-        cp.start()
         a_copies.append(cp)
+
+    for k in range(1, BACK + 1):
+        @pl.when(z + k < NZ)
+        def _():
+            a_copies[k - 1].start()
+
 
     span = 1
     factor = chunk_decay
@@ -227,15 +291,16 @@
 
     lax.fori_loop(0, CHUNK, second_pass, entering, unroll=2)
 
-    for number in (4, 8, 12):
-        wait_w(number)
-    for number, dz in W_NEXT:
-        tile = lax.rem(z + number, NZ)
-        send_w(wbuf.at[tile], tile, dz, (number - dz) % NZ)
+    @pl.when(late)
+    def _():
+        next_tiles(())
 
     carried = jnp.zeros((MODES, CH), F32)
     for k in range(1, BACK + 1):
-        a_copies[k - 1].wait_recv()
+        @pl.when(z >= k)
+        def _():
+            a_copies[k - 1].wait_recv()
+
         ending = seg_ref[jnp.maximum((z - k) * NY + NY - 1, 0)]
         live = jnp.where(jnp.logical_and(z >= k, ending == seg[0]), one, zero)
         weight = jnp.exp(-rate * float(ROWS * (k - 1))) * live
@@ -257,6 +322,10 @@
             recv_sem=x_recv.at[i], device_id=dev(**move), device_id_type=MESH)
         cp.start()
         x_copies.append(cp)
+    @pl.when(jnp.logical_not(late))
+    def _():
+        next_tiles(W_FIRST[3:])
+
     f_copies = []
     for i, dx in enumerate((-1, 1, 2)):
         x_copies[i].wait_recv()
@@ -271,7 +340,7 @@
         cp.wait_recv()
     for number in range(1, NZ):
         if number not in (4, 8, 12):
-            wait_w(number)
+            await_w(number).wait_recv()
 
     def project(at):
         rows = pl.ds(pl.multiple_of(at * TILE, TILE), TILE)
@@ -297,10 +366,16 @@
         own[...] + precv[0].astype(F32) + precv[1].astype(F32) + precv[2].astype(F32)
     ).astype(BF)
 
-    for cp in y_copies + w_copies + a_copies + x_copies + f_copies + p_copies:
+    for cp in y_copies + x_copies + f_copies + p_copies:
         cp.wait_send()
-
-    @pl.when(y == NY - 1)
+    for number in range(1, NZ):
+        await_w(number).wait_send()
+    for k in range(1, BACK + 1):
+        @pl.when(z + k < NZ)
+        def _():
+            a_copies[k - 1].wait_send()
+
+    @pl.when(jnp.logical_and(y == NY - 1, z < NZ - 1))
     def _():
         for t in range(NY):
             rim_copy(t).wait_send()
@@ -310,9 +385,19 @@
     query, key, value, residual, short_taps, decay, residue, skip_gain, segments, out_weight
 ):
     vmem = pl.BlockSpec(memory_space=pltpu.VMEM)
+    hbm = pl.BlockSpec(memory_space=pltpu.HBM)
     smem = pl.BlockSpec(memory_space=pltpu.SMEM)
     dma = pltpu.SemaphoreType.DMA
     scratch = [
+        pltpu.VMEM((TILE, 512), BF),
+        pltpu.VMEM((TILE, 512), BF),
+        pltpu.VMEM((TILE, 512), BF),
+        pltpu.VMEM((TILE, 512), BF),
+        pltpu.VMEM((3, 3, 512), F32),
+        pltpu.VMEM((MODES, 512), F32),
+        pltpu.VMEM((MODES, 512), F32),
+        pltpu.VMEM((1, 512), F32),
+        pltpu.VMEM((64, 512), BF),
         pltpu.VMEM((NY, 3, TILE, CH), BF),
         pltpu.VMEM((NY, 3, TILE, CH), BF),
         pltpu.VMEM((3, 16, CH), BF),
@@ -337,16 +422,17 @@
         pltpu.VMEM((TILE, 512), F32),
         dma((3,)), dma((3,)), dma((NY,)), dma,
         dma((BACK,)), dma((BACK,)), dma((4,)), dma((4,)), dma((3,)), dma((3,)),
-        dma((15,)), dma((NZ,)), dma((3,)), dma((3,)),
+        dma((15,)), dma((NZ,)), dma((3,)), dma((3,)), dma((9,)),
+        pltpu.SemaphoreType.REGULAR, pltpu.SemaphoreType.REGULAR,
     ]
     return pl.pallas_call(
         kernel,
         out_shape=jax.ShapeDtypeStruct((TILE, 512), BF),
-        in_specs=[smem] + [vmem] * 9,
+        in_specs=[smem] + [hbm] * 9,
         out_specs=vmem,
         scratch_shapes=scratch,
         compiler_params=pltpu.CompilerParams(
-            collective_id=0, has_side_effects=True, vmem_limit_bytes=32 * 1024 * 1024),
+            collective_id=0, has_side_effects=True, vmem_limit_bytes=60 * 1024 * 1024),
         name="hyena_block",
     )(segments, query, key, value, residual, short_taps, decay, residue,
       skip_gain.reshape(1, -1), out_weight)

time: 67.1 us -> 57.1 us (0.85)
  the two profiles are of different devices: /device:TPU:1 before, /device:TPU:68 now
where the time goes in v2:
time: 57.1 us; the launch traced here: 56.9 us
  Pallas kernels  55.3 us (97%)
  local copies, waits for them, and re-layouts  1.57 us (3%)
    pallas_call x1, Pallas kernels, per_device(): pl.pallas_call(kernel, out_shape=jax.ShapeDtypeStruct((TILE, 512), BF), i...  55.3 us
    unnamed x1, local copies, waits for them, and re-layouts  1.57 us

profile of v2, /device:TPU:68, one launch (start us, length us, event | category | flops | bytes accessed | tf_op | source)
XLA Modules:
  0.0 56.9 jit_solution(6143934387118947235)
XLA Ops:
  0.0 55.3 %hyena_block.1 = bf16[128,512]{1,0:T(8,128)(2,1)} custom-call(s32[64]{0:T(128)} %seg_ref.1, bf16[128,512]{1,0:T(8,128)(2,1)} %q_hbm.1, bf16[128,512]{1,0:T(8,128)(2,1)} %k_hbm.1, bf16[128,512]{1,0:T(8,128)(2,1)} %v_hbm.1, bf16[128,512]{1,0:T(8,128)(2,1)} %res_hbm.1, f32[3,3,512]{2,1,0:T(4,128)} %taps_hbm.1, f32[16,512]{1,0:T(8,128)} %decay_hbm.1, ...), custom_call_target="tpu_custom_call" | custom-call | tf_op jit(solution)/shard_map/hyena_block/pallas_call | solution.py:428
  55.3 1.6 %copy.12 = bf16[128,512]{1,0:T(8,128)(2,1)} copy(bf16[128,512]{1,0:T(8,128)(2,1)} %hyena_block.1) | data formatting | bytes 262144

commit v3 on v2

--- a/solution.py
+++ b/solution.py
@@ -17,23 +17,30 @@
 CHUNK = ROWS // 8
 BACK = 8
 
-W_FIRST = ((4, 12), (-4, 4), (8, 8), (1, 15), (-1, 1), (2, 14))
-W_NEXT = ((4, 1), (8, 1), (12, 1), (4, -1), (8, -1), (12, -1), (4, 2), (4, -2), (8, -2))
+STEPS = (
+    ((0, (2, -2, 1, -1)),),
+    ((14, (2, 1)), (2, (-2, -1))),
+    ((12, (2, 1)), (4, (-2, -1))),
+    ((10, (2, 1)), (6, (-1,))),
+)
+LATE = {1: (1,), 2: (2,), 3: (3,)}
+EARLY = {1: (1,), 3: (2,), 4: (3,)}
 
 
 def kernel(
     seg_ref, q_hbm, k_hbm, v_hbm, res_hbm, taps_hbm, decay_hbm, residue_hbm, skip_hbm, w_hbm,
     out_ref,
-    q_ref, k_ref, v_ref, res_ref, taps_ref, decay_ref, residue_ref, skip_ref, w_ref,
+    qkv, res_ref, taps_ref, decay_ref, residue_ref, skip_ref, w_ref,
     stage, rbuf, rim, fq, fk, fv, prm, xs, qs, ys, dtab, gtab, atab, ctab, asend, arecv,
-    gbuf, xbuf, wbuf, psend, precv, own,
+    gbuf, xbuf, wbuf, psend, precv, own, sums,
     y_send, y_recv, rim_send, rim_recv, a_send, a_recv, x_send, x_recv, f_send, f_recv,
-    w_send, w_recv, p_send, p_recv, in_sem, go, zgo,
+    w_send, w_recv, p_send, p_recv, in_sem, go, zgo, blocks, plane,
 ):
     inputs = [
         pltpu.make_async_copy(there, ref, in_sem.at[i])
         for i, (there, ref) in enumerate((
-            (q_hbm, q_ref), (k_hbm, k_ref), (v_hbm, v_ref), (w_hbm, w_ref), (decay_hbm, decay_ref),
+            (q_hbm, qkv.at[0:TILE]), (k_hbm, qkv.at[TILE : 2 * TILE]),
+            (v_hbm, qkv.at[2 * TILE : 3 * TILE]), (w_hbm, w_ref), (decay_hbm, decay_ref),
             (residue_hbm, residue_ref), (taps_hbm, taps_ref), (skip_hbm, skip_ref),
             (res_hbm, res_ref)))
     ]
@@ -53,8 +60,8 @@
         )
 
     barrier = pltpu.get_barrier_semaphore()
-    hub = jnp.logical_and(chan == 0, y == 0)
-    hub_pair = jnp.logical_and(chan == 1, y == 0)
+    hub = y == 0
+    hub_pair = y == 1
 
     def greet(sem, where):
         pl.semaphore_signal(sem, inc=1, device_id=where, device_id_type=MESH)
@@ -64,28 +71,20 @@
 
     @pl.when(hub)
     def _():
+        for j in range(1, 2 * NX):
+            greet(barrier, (z * NY, lax.rem(chan + j, 2 * NX)))
         for j in range(NZ):
-            greet(barrier, dev(dz=j, dc=1))
+            greet(barrier, dev(dz=j, toy=1))
 
     @pl.when(jnp.logical_not(hub))
     def _():
-        greet(barrier, (z * NY, 0))
+        greet(barrier, dev(toy=0))
         for j in range(1, NZ):
             greet(barrier, dev(dz=j))
 
     @pl.when(y != NY - 1)
     def _():
         greet(barrier, dev(dz=-1, toy=NY - 1))
-
-    src = lax.broadcasted_iota(jnp.int32, (512, 512), 0)
-    dst = lax.broadcasted_iota(jnp.int32, (512, 512), 1)
-    wanted = ((dst >> 6) & 1) * 256 + (dst >> 7) * 64 + (dst & 63)
-    perm = jnp.where(src == wanted, 1.0, 0.0).astype(BF)
-    for s, ref in enumerate((q_ref, k_ref, v_ref)):
-        inputs[s].wait()
-        moved = jnp.dot(ref[...], perm, preferred_element_type=F32).astype(BF)
-        for t in range(NY):
-            stage[t, s] = moved[:, t * CH : (t + 1) * CH]
 
     def send_w(source, tile, dz, number):
         at = (number - 1) % NZ
@@ -98,7 +97,7 @@
             src_ref=w_ref, dst_ref=wbuf.at[lax.rem(z + number, NZ)], send_sem=w_send.at[number - 1],
             recv_sem=w_recv.at[number], device_id=dev(dz=1), device_id_type=MESH)
 
-    def planes(moves):
+    def planes():
         @pl.when(jnp.logical_not(hub))
         def _():
             pl.semaphore_wait(
@@ -106,36 +105,55 @@
 
         @pl.when(hub_pair)
         def _():
-            greet(zgo, dev(dc=1))
+            greet(zgo, dev(toy=0))
 
         @pl.when(hub)
         def _():
             pl.semaphore_wait(zgo, 1)
 
-        for dz, number in moves:
-            send_w(w_ref, z, dz, number)
-
-    def next_tiles(moves):
-        for dz, number in moves:
-            send_w(w_ref, z, dz, number)
-        for number in (4, 8, 12):
-            await_w(number).wait_recv()
-        for number, dz in W_NEXT:
+    late = z >= NZ // 2
+    waited = [number for step in STEPS for number, _ in step if number]
+
+    def pass_on(step):
+        for number, moves in STEPS[step]:
             tile = lax.rem(z + number, NZ)
-            send_w(wbuf.at[tile], tile, dz, (number - dz) % NZ)
-
-    late = z >= NZ // 2
-    inputs[3].wait()
+            if number:
+                await_w(number).wait_recv()
+            for dz in moves:
+                send_w(wbuf.at[tile] if number else w_ref, tile, dz, (number - dz) % NZ)
+
+    def w_place(place):
+        for when, steps in ((late, LATE), (jnp.logical_not(late), EARLY)):
+            if place in steps:
+                @pl.when(when)
+                def _():
+                    for step in steps[place]:
+                        pass_on(step)
+
+    src = lax.broadcasted_iota(jnp.int32, (512, 512), 0)
+    dst = lax.broadcasted_iota(jnp.int32, (512, 512), 1)
+    wanted = ((dst >> 6) & 1) * 256 + (dst >> 7) * 64 + (dst & 63)
+    perm = jnp.where(src == wanted, 1.0, 0.0).astype(BF)
 
     @pl.when(hub)
     def _():
-        pl.semaphore_wait(barrier, NY * 2 * NX - 1)
-        for j in range(NY * 2 * NX - 1, 0, -1):
-            greet(go, (z * NY + j // (2 * NX), j % (2 * NX)))
+        pl.semaphore_wait(barrier, NY - 1 + 2 * NX - 1)
+        for j in range(1, NY):
+            greet(go, dev(toy=j))
+        for j in range(1, 2 * NX):
+            greet(blocks, (z * NY, lax.rem(chan + j, 2 * NX)))
+
+    for i in range(4):
+        inputs[i].wait()
+    moved = jnp.dot(qkv[...], perm, preferred_element_type=F32).astype(BF)
+    for s in range(3):
+        for t in range(NY):
+            stage[t, s] = moved[s * TILE : (s + 1) * TILE, t * CH : (t + 1) * CH]
 
     @pl.when(late)
     def _():
-        planes(W_FIRST)
+        planes()
+        pass_on(0)
 
     @pl.when(jnp.logical_not(hub))
     def _():
@@ -157,12 +175,23 @@
 
     @pl.when(jnp.logical_not(late))
     def _():
-        planes(W_FIRST[:3])
+        planes()
+        pass_on(0)
 
     @pl.when(jnp.logical_and(y == NY - 1, z < NZ - 1))
     def _():
         for t in range(NY):
             rim_copy(t).start()
+
+    @pl.when(hub)
+    def _():
+        pl.semaphore_wait(blocks, 2 * NX - 1)
+        for j in range(1, NY):
+            greet(plane, dev(toy=j))
+
+    @pl.when(jnp.logical_not(hub))
+    def _():
+        pl.semaphore_wait(plane, 1)
 
     wbuf[z] = w_ref[...]
 
@@ -212,6 +241,8 @@
     ctab[...] = gain8 * jnp.exp(-rate8 * (CHUNK * subf)[None]) * by_tile(starts)[None]
     chunk_decay = jnp.exp(-rate8 * float(CHUNK)) * joined[None]
 
+    w_place(1)
+
     streams = (fq, fk, fv)
     here = pl.multiple_of(8 + y * TILE, 8)
     for s in range(3):
@@ -274,6 +305,8 @@
             a_copies[k - 1].start()
 
 
+    w_place(2)
+
     span = 1
     factor = chunk_decay
     state = h
@@ -291,9 +324,7 @@
 
     lax.fori_loop(0, CHUNK, second_pass, entering, unroll=2)
 
-    @pl.when(late)
-    def _():
-        next_tiles(())
+    w_place(3)
 
     carried = jnp.zeros((MODES, CH), F32)
     for k in range(1, BACK + 1):
@@ -313,58 +344,73 @@
         return e
 
     lax.fori_loop(0, CHUNK, third_pass, ctab[...] * carried[:, None, :], unroll=2)
-    xbuf[chan] = gbuf[...].astype(BF)
-
+    for part in range(2):
+        for t in range(NY):
+            xbuf[part, chan, t * CHUNK : (t + 1) * CHUNK] = gbuf[
+                (2 * t + part) * CHUNK : (2 * t + part + 1) * CHUNK].astype(BF)
+
+    x_moves = (dict(dx=2), dict(dx=1), dict(dx=-1), dict(dc=1))
     x_copies = []
-    for i, move in enumerate((dict(dx=1), dict(dx=-1), dict(dx=2), dict(dc=1))):
-        cp = pltpu.make_async_remote_copy(
-            src_ref=xbuf.at[chan], dst_ref=xbuf.at[chan], send_sem=x_send.at[i],
-            recv_sem=x_recv.at[i], device_id=dev(**move), device_id_type=MESH)
-        cp.start()
-        x_copies.append(cp)
-    @pl.when(jnp.logical_not(late))
-    def _():
-        next_tiles(W_FIRST[3:])
+    for part in range(2):
+        for i, move in enumerate(x_moves):
+            cp = pltpu.make_async_remote_copy(
+                src_ref=xbuf.at[part, chan], dst_ref=xbuf.at[part, chan],
+                send_sem=x_send.at[part, i], recv_sem=x_recv.at[part, i], device_id=dev(**move),
+                device_id_type=MESH)
+            cp.start()
+            x_copies.append(cp)
+    w_place(4)
 
     f_copies = []
-    for i, dx in enumerate((-1, 1, 2)):
-        x_copies[i].wait_recv()
-        slot = lax.rem(x + dx + NX, NX) * 2 + core
-        cp = pltpu.make_async_remote_copy(
-            src_ref=xbuf.at[slot], dst_ref=xbuf.at[slot], send_sem=f_send.at[i],
-            recv_sem=f_recv.at[i], device_id=dev(dc=1), device_id_type=MESH)
-        cp.start()
-        f_copies.append(cp)
-    x_copies[3].wait_recv()
-    for cp in f_copies:
-        cp.wait_recv()
-    for number in range(1, NZ):
-        if number not in (4, 8, 12):
-            await_w(number).wait_recv()
-
-    def project(at):
-        rows = pl.ds(pl.multiple_of(at * TILE, TILE), TILE)
-        total = jnp.zeros((TILE, 512), F32)
+    p_copies = []
+    for part in range(2):
+        for i, dx in ((1, -1), (2, 1), (0, 2)):
+            x_copies[4 * part + i].wait_recv()
+            slot = lax.rem(x + dx + NX, NX) * 2 + core
+            cp = pltpu.make_async_remote_copy(
+                src_ref=xbuf.at[part, slot], dst_ref=xbuf.at[part, slot],
+                send_sem=f_send.at[part, i], recv_sem=f_recv.at[part, i], device_id=dev(dc=1),
+                device_id_type=MESH)
+            cp.start()
+            f_copies.append(cp)
+        if part == 0:
+            w_place(5)
+        x_copies[4 * part + 3].wait_recv()
+        for i in range(3):
+            f_copies[3 * part + i].wait_recv()
+        if part == 0:
+            for number in range(1, NZ):
+                if number not in waited:
+                    await_w(number).wait_recv()
+
+        total = jnp.zeros((NY * CHUNK, 512), F32)
         for p in range(NX):
-            left = jnp.concatenate([xbuf[2 * p, rows], xbuf[2 * p + 1, rows]], axis=1)
+            left = jnp.concatenate([xbuf[part, 2 * p], xbuf[part, 2 * p + 1]], axis=1)
             right = wbuf[4 * p : 4 * p + 4].reshape(256, 512)
             total = total + jnp.dot(left, right, preferred_element_type=F32)
-        return total
-
-    p_copies = []
-    for j in range(1, NY):
-        psend[j - 1] = project(lax.rem(y + j, NY)).astype(BF)
-        cp = pltpu.make_async_remote_copy(
-            src_ref=psend.at[j - 1], dst_ref=precv.at[j - 1], send_sem=p_send.at[j - 1],
-            recv_sem=p_recv.at[j - 1], device_id=dev(dy=j), device_id_type=MESH)
-        cp.start()
-        p_copies.append(cp)
-    own[...] = project(y) + res_ref[...].astype(F32)
-    for j in range(NY - 1):
-        p_copies[j].wait_recv()
-    out_ref[...] = (
-        own[...] + precv[0].astype(F32) + precv[1].astype(F32) + precv[2].astype(F32)
-    ).astype(BF)
+        sums[part] = total
+        for j in (2, 1, 3):
+            rows = pl.ds(pl.multiple_of(lax.rem(y + j, NY) * CHUNK, CHUNK), CHUNK)
+            psend[part, j - 1] = sums[part, rows].astype(BF)
+            cp = pltpu.make_async_remote_copy(
+                src_ref=psend.at[part, j - 1], dst_ref=precv.at[part, j - 1],
+                send_sem=p_send.at[part, j - 1], recv_sem=p_recv.at[part, j - 1],
+                device_id=dev(dy=j), device_id_type=MESH)
+            cp.start()
+            p_copies.append(cp)
+
+    for part in range(2):
+        rows = pl.ds(pl.multiple_of(y * CHUNK, CHUNK), CHUNK)
+        mine_out = slice(part * CHUNK, (part + 1) * CHUNK)
+        own[mine_out] = sums[part, rows] + res_ref[mine_out].astype(F32)
+    for part in range(2):
+        mine_out = slice(part * CHUNK, (part + 1) * CHUNK)
+        for j in range(3):
+            p_copies[3 * part + j].wait_recv()
+        out_ref[mine_out] = (
+            own[mine_out] + precv[part, 0].astype(F32) + precv[part, 1].astype(F32)
+            + precv[part, 2].astype(F32)
+        ).astype(BF)
 
     for cp in y_copies + x_copies + f_copies + p_copies:
         cp.wait_send()
@@ -389,9 +435,7 @@
     smem = pl.BlockSpec(memory_space=pltpu.SMEM)
     dma = pltpu.SemaphoreType.DMA
     scratch = [
-        pltpu.VMEM((TILE, 512), BF),
-        pltpu.VMEM((TILE, 512), BF),
-        pltpu.VMEM((TILE, 512), BF),
+        pltpu.VMEM((3 * TILE, 512), BF),
         pltpu.VMEM((TILE, 512), BF),
         pltpu.VMEM((3, 3, 512), F32),
         pltpu.VMEM((MODES, 512), F32),
@@ -415,14 +459,16 @@
         pltpu.VMEM((MODES, CH), BF),
         pltpu.VMEM((BACK, MODES, CH), BF),
         pltpu.VMEM((ROWS, CH), F32),
-        pltpu.VMEM((2 * NX, ROWS, CH), BF),
+        pltpu.VMEM((2, 2 * NX, ROWS // 2, CH), BF),
         pltpu.VMEM((NZ, 64, 512), BF),
-        pltpu.VMEM((NY - 1, TILE, 512), BF),
-        pltpu.VMEM((NY - 1, TILE, 512), BF),
+        pltpu.VMEM((2, NY - 1, CHUNK, 512), BF),
+        pltpu.VMEM((2, NY - 1, CHUNK, 512), BF),
         pltpu.VMEM((TILE, 512), F32),
+        pltpu.VMEM((2, ROWS // 2, 512), F32),
         dma((3,)), dma((3,)), dma((NY,)), dma,
-        dma((BACK,)), dma((BACK,)), dma((4,)), dma((4,)), dma((3,)), dma((3,)),
-        dma((15,)), dma((NZ,)), dma((3,)), dma((3,)), dma((9,)),
+        dma((BACK,)), dma((BACK,)), dma((2, 4)), dma((2, 4)), dma((2, 3)), dma((2, 3)),
+        dma((15,)), dma((NZ,)), dma((2, 3)), dma((2, 3)), dma((9,)),
+        pltpu.SemaphoreType.REGULAR, pltpu.SemaphoreType.REGULAR,
         pltpu.SemaphoreType.REGULAR, pltpu.SemaphoreType.REGULAR,
     ]
     return pl.pallas_call(

time: 57.1 us -> 47.9 us (0.84)
  the two profiles are of different devices: /device:TPU:68 before, /device:TPU:1 now
where the time goes in v3:
time: 47.9 us; the launch traced here: 47.5 us
  Pallas kernels  45.9 us (96%)
  local copies, waits for them, and re-layouts  1.57 us (3%)
    pallas_call x1, Pallas kernels, per_device(): pl.pallas_call(kernel, out_shape=jax.ShapeDtypeStruct((TILE, 512), BF), i...  45.9 us
    unnamed x1, local copies, waits for them, and re-layouts  1.57 us

profile of v3, /device:TPU:1, one launch (start us, length us, event | category | flops | bytes accessed | tf_op | source)
XLA Modules:
  0.0 47.5 jit_solution(15384729150047166472)
XLA Ops:
  0.0 45.9 %hyena_block.1 = bf16[128,512]{1,0:T(8,128)(2,1)} custom-call(s32[64]{0:T(128)} %seg_ref.1, bf16[128,512]{1,0:T(8,128)(2,1)} %q_hbm.1, bf16[128,512]{1,0:T(8,128)(2,1)} %k_hbm.1, bf16[128,512]{1,0:T(8,128)(2,1)} %v_hbm.1, bf16[128,512]{1,0:T(8,128)(2,1)} %res_hbm.1, f32[3,3,512]{2,1,0:T(4,128)} %taps_hbm.1, f32[16,512]{1,0:T(8,128)} %decay_hbm.1, ...), custom_call_target="tpu_custom_call" | custom-call | tf_op jit(solution)/shard_map/hyena_block/pallas_call | solution.py:474
  46.0 1.6 %copy.12 = bf16[128,512]{1,0:T(8,128)(2,1)} copy(bf16[128,512]{1,0:T(8,128)(2,1)} %hyena_block.1) | data formatting | bytes 262144

commit v4 on v3

--- a/solution.py
+++ b/solution.py
@@ -18,34 +18,37 @@
 BACK = 8
 
 STEPS = (
-    ((0, (2, -2, 1, -1)),),
-    ((14, (2, 1)), (2, (-2, -1))),
-    ((12, (2, 1)), (4, (-2, -1))),
-    ((10, (2, 1)), (6, (-1,))),
+    ((0, (2, -2)),),
+    ((14, (2,)), (2, (-2,))),
+    ((12, (2,)), (4, (-2,))),
+    ((10, (2,)), (6, ())),
+    ((0, (1, -1)),),
+    ((14, (1,)), (2, (-1,))),
+    ((12, (1,)), (4, (-1,))),
+    ((10, (1,)), (6, (-1,))),
 )
-LATE = {1: (1,), 2: (2,), 3: (3,)}
-EARLY = {1: (1,), 3: (2,), 4: (3,)}
+LATE = {1: (1, 4), 2: (2, 5, 6), 3: (3, 7)}
+EARLY = {1: (1,), 3: (2, 6, 4, 5), 4: (3, 7)}
 
 
 def kernel(
     seg_ref, q_hbm, k_hbm, v_hbm, res_hbm, taps_hbm, decay_hbm, residue_hbm, skip_hbm, w_hbm,
-    out_ref,
-    qkv, res_ref, taps_ref, decay_ref, residue_ref, skip_ref, w_ref,
+    out_hbm,
+    out_ref, qkv, res_ref, taps_ref, decay_ref, residue_ref, skip_ref, w_ref,
     stage, rbuf, rim, fq, fk, fv, prm, xs, qs, ys, dtab, gtab, atab, ctab, asend, arecv,
     gbuf, xbuf, wbuf, psend, precv, own, sums,
     y_send, y_recv, rim_send, rim_recv, a_send, a_recv, x_send, x_recv, f_send, f_recv,
-    w_send, w_recv, p_send, p_recv, in_sem, go, zgo, blocks, plane,
+    w_send, w_recv, p_send, p_recv, in_sem, out_sem, go, zgo, blocks, plane,
 ):
     inputs = [
         pltpu.make_async_copy(there, ref, in_sem.at[i])
         for i, (there, ref) in enumerate((
-            (q_hbm, qkv.at[0:TILE]), (k_hbm, qkv.at[TILE : 2 * TILE]),
-            (v_hbm, qkv.at[2 * TILE : 3 * TILE]), (w_hbm, w_ref), (decay_hbm, decay_ref),
+            (w_hbm, w_ref), (q_hbm, qkv.at[0:TILE]), (k_hbm, qkv.at[TILE : 2 * TILE]),
+            (v_hbm, qkv.at[2 * TILE : 3 * TILE]), (decay_hbm, decay_ref),
             (residue_hbm, residue_ref), (taps_hbm, taps_ref), (skip_hbm, skip_ref),
             (res_hbm, res_ref)))
     ]
-    for cp in inputs:
-        cp.start()
+    inputs[0].start()
 
     seq = lax.axis_index("seq")
     chan = lax.axis_index("chan")
@@ -86,6 +89,9 @@
     def _():
         greet(barrier, dev(dz=-1, toy=NY - 1))
 
+    for cp in inputs[1:]:
+        cp.start()
+
     def send_w(source, tile, dz, number):
         at = (number - 1) % NZ
         pltpu.make_async_remote_copy(
@@ -112,12 +118,12 @@
             pl.semaphore_wait(zgo, 1)
 
     late = z >= NZ // 2
-    waited = [number for step in STEPS for number, _ in step if number]
+    waited = (14, 2, 12, 4, 10, 6)
 
     def pass_on(step):
         for number, moves in STEPS[step]:
             tile = lax.rem(z + number, NZ)
-            if number:
+            if 0 < step < 4:
                 await_w(number).wait_recv()
             for dz in moves:
                 send_w(wbuf.at[tile] if number else w_ref, tile, dz, (number - dz) % NZ)
@@ -143,30 +149,33 @@
         for j in range(1, 2 * NX):
             greet(blocks, (z * NY, lax.rem(chan + j, 2 * NX)))
 
-    for i in range(4):
+    inputs[0].wait()
+
+    @pl.when(late)
+    def _():
+        planes()
+        pass_on(0)
+
+    for i in range(1, 4):
         inputs[i].wait()
     moved = jnp.dot(qkv[...], perm, preferred_element_type=F32).astype(BF)
     for s in range(3):
         for t in range(NY):
             stage[t, s] = moved[s * TILE : (s + 1) * TILE, t * CH : (t + 1) * CH]
 
-    @pl.when(late)
-    def _():
-        planes()
-        pass_on(0)
-
     @pl.when(jnp.logical_not(hub))
     def _():
         pl.semaphore_wait(go, 1)
 
     y_copies = []
-    for j in range(1, NY):
-        to = lax.rem(y + j, NY)
-        cp = pltpu.make_async_remote_copy(
-            src_ref=stage.at[to], dst_ref=rbuf.at[y], send_sem=y_send.at[j - 1],
-            recv_sem=y_recv.at[j - 1], device_id=dev(dy=j), device_id_type=MESH)
-        cp.start()
-        y_copies.append(cp)
+    for group, of in enumerate((slice(1, 3), slice(0, 1))):
+        for j in range(1, NY):
+            to = lax.rem(y + j, NY)
+            cp = pltpu.make_async_remote_copy(
+                src_ref=stage.at[to, of], dst_ref=rbuf.at[y, of], send_sem=y_send.at[group, j - 1],
+                recv_sem=y_recv.at[group, j - 1], device_id=dev(dy=j), device_id_type=MESH)
+            cp.start()
+            y_copies.append(cp)
 
     def rim_copy(t):
         return pltpu.make_async_remote_copy(
@@ -244,15 +253,20 @@
     w_place(1)
 
     streams = (fq, fk, fv)
-    here = pl.multiple_of(8 + y * TILE, 8)
-    for s in range(3):
-        streams[s][pl.ds(here, TILE)] = stage[y, s].astype(F32)
-    for j in range(1, NY):
-        y_copies[j - 1].wait_recv()
-        origin = lax.rem(y - j + NY, NY)
-        at = pl.multiple_of(8 + origin * TILE, 8)
-        for s in range(3):
-            streams[s][pl.ds(at, TILE)] = rbuf[origin, s].astype(F32)
+
+    def fill(group, of):
+        here = pl.multiple_of(8 + y * TILE, 8)
+        for s in of:
+            streams[s][pl.ds(here, TILE)] = stage[y, s].astype(F32)
+        for j in range(1, NY):
+            y_copies[group * (NY - 1) + j - 1].wait_recv()
+            origin = lax.rem(y - j + NY, NY)
+            at = pl.multiple_of(8 + origin * TILE, 8)
+            for s in of:
+                streams[s][pl.ds(at, TILE)] = rbuf[origin, s].astype(F32)
+
+    fill(0, (1, 2))
+
     @pl.when(z > 0)
     def _():
         rim_copy(0).wait_recv()
@@ -263,30 +277,28 @@
     def load(s, b):
         return streams[s][pl.ds(8 + b, 8, stride=CHUNK), :]
 
-    def mix(now, last, older):
-        out = []
-        for s in range(3):
-            out.append(now[s] * taps[s][0] + last[s] * taps[s][1] + older[s] * taps[s][2])
-        return out[0], (out[1] * out[2]).astype(BF).astype(F32)
-
-    def keep(b, mixed):
-        qs[b] = mixed[0]
-        xs[b] = mixed[1]
-        return mixed[1]
-
-    m2 = [load(s, -2) * joined for s in range(3)]
-    m1 = [load(s, -1) * joined for s in range(3)]
-    f0 = [load(s, 0) for s in range(3)]
-    f1 = [load(s, 1) for s in range(3)]
-    d16 = dtab[...]
-    x0 = keep(0, mix(f0, m1, m2))
-    x1 = keep(1, mix(f1, f0, m1))
-    h = x0[None] * d16 + x1[None]
+    def short(s, now, last, older):
+        return now * taps[s][0] + last * taps[s][1] + older * taps[s][2]
+
+    def start(of):
+        return (
+            [load(s, -2) * joined for s in of], [load(s, -1) * joined for s in of],
+            [load(s, 0) for s in of], [load(s, 1) for s in of])
+
+    def mix(b, now, last, older):
+        ks = short(1, now[0], last[0], older[0])
+        vs = short(2, now[1], last[1], older[1])
+        xb = (ks * vs).astype(BF).astype(F32)
+        xs[b] = xb
+        return xb
+
+    m2, m1, f0, f1 = start((1, 2))
+    h = mix(0, f0, m1, m2)[None] * dtab[...] + mix(1, f1, f0, m1)[None]
 
     def first_pass(b, carry):
         h, last, older = carry
-        now = [load(s, b) for s in range(3)]
-        xb = keep(b, mix(now, last, older))
+        now = [load(s, b) for s in (1, 2)]
+        xb = mix(b, now, last, older)
         return (h * dtab[...] + xb[None], now, last)
 
     h, _, _ = lax.fori_loop(2, CHUNK, first_pass, (h, f1, f0), unroll=2)
@@ -316,13 +328,25 @@
         span *= 2
     entering = jnp.where(sub[None] >= 1, pltpu.roll(state, 1, 1) * joined[None], zero)
 
-    def second_pass(b, h):
+    fill(1, (0,))
+    m2, m1, f0, f1 = start((0,))
+
+    def convolve(b, h, now, last, older):
+        qs[b] = short(0, now, last, older)
         xb = xs[b]
         h = h * dtab[...] + xb[None]
         ys[b] = skip * xb + jnp.sum(h * gtab[...], axis=0)
         return h
 
-    lax.fori_loop(0, CHUNK, second_pass, entering, unroll=2)
+    h = convolve(0, entering, f0[0], m1[0], m2[0])
+    h = convolve(1, h, f1[0], f0[0], m1[0])
+
+    def second_pass(b, carry):
+        h, last, older = carry
+        now = load(0, b)
+        return (convolve(b, h, now, last, older), now, last)
+
+    lax.fori_loop(2, CHUNK, second_pass, (h, f1[0], f0[0]), unroll=2)
 
     w_place(3)
 
@@ -337,6 +361,7 @@
         weight = jnp.exp(-rate * float(ROWS * (k - 1))) * live
         carried = carried + weight * arecv[k - 1].astype(F32)
 
+    w_place(35)
     def third_pass(b, e):
         e = e * dtab[...]
         long_out = (ys[b] + jnp.sum(e, axis=0)).astype(BF).astype(F32)
@@ -403,6 +428,7 @@
         rows = pl.ds(pl.multiple_of(y * CHUNK, CHUNK), CHUNK)
         mine_out = slice(part * CHUNK, (part + 1) * CHUNK)
         own[mine_out] = sums[part, rows] + res_ref[mine_out].astype(F32)
+    outputs = []
     for part in range(2):
         mine_out = slice(part * CHUNK, (part + 1) * CHUNK)
         for j in range(3):
@@ -411,7 +437,12 @@
             own[mine_out] + precv[part, 0].astype(F32) + precv[part, 1].astype(F32)
             + precv[part, 2].astype(F32)
         ).astype(BF)
-
+        outputs.append(pltpu.make_async_copy(
+            out_ref.at[mine_out], out_hbm.at[mine_out], out_sem.at[part]))
+        outputs[part].start()
+
+    for cp in outputs:
+        cp.wait()
     for cp in y_copies + x_copies + f_copies + p_copies:
         cp.wait_send()
     for number in range(1, NZ):
@@ -435,6 +466,7 @@
     smem = pl.BlockSpec(memory_space=pltpu.SMEM)
     dma = pltpu.SemaphoreType.DMA
     scratch = [
+        pltpu.VMEM((TILE, 512), BF),
         pltpu.VMEM((3 * TILE, 512), BF),
         pltpu.VMEM((TILE, 512), BF),
         pltpu.VMEM((3, 3, 512), F32),
@@ -445,9 +477,9 @@
         pltpu.VMEM((NY, 3, TILE, CH), BF),
         pltpu.VMEM((NY, 3, TILE, CH), BF),
         pltpu.VMEM((3, 16, CH), BF),
-        pltpu.VMEM((8 + ROWS, CH), F32),
-        pltpu.VMEM((8 + ROWS, CH), F32),
-        pltpu.VMEM((8 + ROWS, CH), F32),
+        pltpu.VMEM((8 + ROWS + CHUNK, CH), F32),
+        pltpu.VMEM((8 + ROWS + CHUNK, CH), F32),
+        pltpu.VMEM((8 + ROWS + CHUNK, CH), F32),
         pltpu.VMEM((48, 512), F32),
         pltpu.VMEM((CHUNK, 8, CH), F32),
         pltpu.VMEM((CHUNK, 8, CH), F32),
@@ -458,16 +490,16 @@
         pltpu.VMEM((MODES, 8, CH), F32),
         pltpu.VMEM((MODES, CH), BF),
         pltpu.VMEM((BACK, MODES, CH), BF),
-        pltpu.VMEM((ROWS, CH), F32),
+        pltpu.VMEM((ROWS + CHUNK, CH), F32),
         pltpu.VMEM((2, 2 * NX, ROWS // 2, CH), BF),
         pltpu.VMEM((NZ, 64, 512), BF),
         pltpu.VMEM((2, NY - 1, CHUNK, 512), BF),
         pltpu.VMEM((2, NY - 1, CHUNK, 512), BF),
         pltpu.VMEM((TILE, 512), F32),
         pltpu.VMEM((2, ROWS // 2, 512), F32),
-        dma((3,)), dma((3,)), dma((NY,)), dma,
+        dma((2, 3)), dma((2, 3)), dma((NY,)), dma,
         dma((BACK,)), dma((BACK,)), dma((2, 4)), dma((2, 4)), dma((2, 3)), dma((2, 3)),
-        dma((15,)), dma((NZ,)), dma((2, 3)), dma((2, 3)), dma((9,)),
+        dma((15,)), dma((NZ,)), dma((2, 3)), dma((2, 3)), dma((9,)), dma((2,)),
         pltpu.SemaphoreType.REGULAR, pltpu.SemaphoreType.REGULAR,
         pltpu.SemaphoreType.REGULAR, pltpu.SemaphoreType.REGULAR,
     ]
@@ -475,7 +507,7 @@
         kernel,
         out_shape=jax.ShapeDtypeStruct((TILE, 512), BF),
         in_specs=[smem] + [hbm] * 9,
-        out_specs=vmem,
+        out_specs=hbm,
         scratch_shapes=scratch,
         compiler_params=pltpu.CompilerParams(
             collective_id=0, has_side_effects=True, vmem_limit_bytes=60 * 1024 * 1024),

time: 47.9 us -> 47.7 us (level)
  no operation moved by 1% of the time
where the time goes in v4:
time: 47.7 us; the launch traced here: 47.6 us
  Pallas kernels  46 us (96%)
  local copies, waits for them, and re-layouts  1.57 us (3%)
    pallas_call x1, Pallas kernels, per_device(): pl.pallas_call(kernel, out_shape=jax.ShapeDtypeStruct((TILE, 512), BF), i...  46 us
    unnamed x1, local copies, waits for them, and re-layouts  1.57 us

profile of v4, /device:TPU:1, one launch (start us, length us, event | category | flops | bytes accessed | tf_op | source)
XLA Modules:
  0.0 47.6 jit_solution(3525856609062463038)
XLA Ops:
  0.0 46.0 %hyena_block.1 = bf16[128,512]{1,0:T(8,128)(2,1)} custom-call(s32[64]{0:T(128)} %seg_ref.1, bf16[128,512]{1,0:T(8,128)(2,1)} %q_hbm.1, bf16[128,512]{1,0:T(8,128)(2,1)} %k_hbm.1, bf16[128,512]{1,0:T(8,128)(2,1)} %v_hbm.1, bf16[128,512]{1,0:T(8,128)(2,1)} %res_hbm.1, f32[3,3,512]{2,1,0:T(4,128)} %taps_hbm.1, f32[16,512]{1,0:T(8,128)} %decay_hbm.1, ...), custom_call_target="tpu_custom_call" | custom-call | tf_op jit(solution)/shard_map/hyena_block/pallas_call | solution.py:506
  46.0 1.6 %copy.12 = bf16[128,512]{1,0:T(8,128)(2,1)} copy(bf16[128,512]{1,0:T(8,128)(2,1)} %hyena_block.1) | data formatting | bytes 262144
